TPU v7x, 256 devices: a whole 4x4x8 slice. The times are simulated.
256 devices in a mesh: tensor: 32 (over x, z), dp: 8 (over y, core).
Axes of the slice: x: 4, y: 4, z: 8, core: 2. Of those that a mesh axis runs over, the one named last changes fastest.
Arguments:
- hidden: bfloat16 [8192, 15360], P('dp', 'tensor'), parts along dimension 0, may hold values from -6 to 6
- residual: bfloat16 [8192, 8192], P(('dp', 'tensor')), parts along dimension 0, may hold values from -24 to 24
- down_weight: bfloat16 [15360, 8192], P('tensor'), may hold values from -0.046875 to 0.046875
- norm_gain: bfloat16 [8192], replicated, may hold values from 0.099609375 to 1.8984375
- query_codes: bfloat16 [8192, 4096], P(None, 'tensor'), may hold values from -4 to 4
- query_scales: bfloat16 [64, 4096], P(None, 'tensor'), may hold values from 0.0010986328 to 0.0043945312
- pair_codes: bfloat16 [2, 8192, 1024], P(None, None, 'tensor'), may hold values from -4 to 4
- pair_scales: bfloat16 [2, 64, 1024], P(None, None, 'tensor'), may hold values from 0.0010986328 to 0.0043945312
- input_groups: int32 [8192], replicated, may hold values from 0 to 63, as said below
- query_bias: bfloat16 [4096], P('tensor'), may hold values from -3 to 3
- pair_bias: bfloat16 [2, 1024], P(None, 'tensor'), may hold values from -3 to 3
Outputs:
- new_residual: bfloat16 [8192, 8192], P(('dp', 'tensor')), parts along dimension 0
- queries: bfloat16 [8192, 4096], P('dp', 'tensor'), parts along dimension 0
- key_values: bfloat16 [2, 8192, 1024], P(None, 'dp', 'tensor'), parts along dimension 1
There are 8 independent parts, one for each index of `dp`. A program takes and returns all parts, laid end to end along the dimension named above; an argument that names none is the same for every part. Nothing has to cross between parts.
Inputs may be any that keep to these rules, and one draw needn't show every extreme that they name: `input_groups`: each value is the quantization group of one model feature; every group of 0 to 63 holds exactly 128 features.
All inputs are finite; a program needn't handle non-finite values.
Results may differ from a plain program's by a relative error of at most 0.02.
Values may be sent and summed in bfloat16 or wider, within the bound.
A program may use at most 192 MiB of HBM per device.

v0:
```python
import jax
import jax.numpy as jnp
from jax import lax
from jax.sharding import PartitionSpec as P


def dequant(codes, selector, scales):
    scale_rows = jnp.dot(selector, scales, preferred_element_type=jnp.float32)
    return (codes.astype(jnp.float32) * scale_rows).astype(jnp.bfloat16)


def per_device(
    hidden,
    residual,
    down_weight,
    norm_gain,
    query_codes,
    query_scales,
    pair_codes,
    pair_scales,
    input_groups,
    query_bias,
    pair_bias,
):
    own_tokens = residual.shape[0]
    own_start = lax.axis_index("tensor") * own_tokens
    group_count = query_scales.shape[0]
    selector = (input_groups[:, None] == jnp.arange(group_count, dtype=jnp.int32)[None, :]).astype(
        jnp.bfloat16
    )
    query_weight = dequant(query_codes, selector, query_scales)
    key_weight = dequant(pair_codes[0], selector, pair_scales[0])
    value_weight = dequant(pair_codes[1], selector, pair_scales[1])
    joined = jnp.concatenate([query_weight, key_weight, value_weight], axis=1)
    query_width = query_weight.shape[1]
    key_width = key_weight.shape[1]
    gain_wide = norm_gain.astype(jnp.float32)
    partial_value = jnp.dot(hidden, down_weight, preferred_element_type=jnp.float32)
    own_rows = lax.dynamic_slice_in_dim(partial_value, own_start, own_tokens, 0) + residual.astype(
        jnp.float32
    )
    partial_value = lax.dynamic_update_slice_in_dim(partial_value, own_rows, own_start, 0)
    summed = lax.psum(partial_value.astype(jnp.bfloat16), "tensor")
    new_residual = lax.dynamic_slice_in_dim(summed, own_start, own_tokens, 0)
    widened = summed.astype(jnp.float32)
    scaled = widened * lax.rsqrt(jnp.mean(widened * widened, axis=1, keepdims=True) + 1e-06)
    projected = jnp.dot(
        (scaled * gain_wide).astype(jnp.bfloat16), joined, preferred_element_type=jnp.float32
    )
    queries = (projected[:, :query_width] + query_bias.astype(jnp.float32)).astype(jnp.bfloat16)
    keys_out = projected[:, query_width : query_width + key_width] + pair_bias[0].astype(
        jnp.float32
    )
    values_out = projected[:, query_width + key_width :] + pair_bias[1].astype(jnp.float32)
    key_values = jnp.stack([keys_out, values_out]).astype(jnp.bfloat16)
    return (new_residual, queries, key_values)


def solution(mesh):
    in_specs = (
        P("dp", "tensor"),
        P(("dp", "tensor"), None),
        P("tensor", None),
        P(),
        P(None, "tensor"),
        P(None, "tensor"),
        P(None, None, "tensor"),
        P(None, None, "tensor"),
        P(),
        P("tensor"),
        P(None, "tensor"),
    )
    out_specs = (P(("dp", "tensor"), None), P("dp", "tensor"), P(None, "dp", "tensor"))
    return jax.shard_map(
        per_device, mesh=mesh, in_specs=in_specs, out_specs=out_specs, check_vma=False
    )
```

profile of v0, /device:TPU:8, one launch (start us, length us, event | category | flops | bytes accessed | tf_op | source)
XLA Modules:
  0.0 404.3 jit_solution(13393644451476029577)
XLA Ops:
  7.2 0.0 copy-start
  7.2 0.0 all-reduce.2.cloned.1.call-start
  7.2 1.1 copy-done
  8.4 0.0 copy-start.5
  8.4 18.6 %fusion.28 = f32[1024,8192]{1,0:T(8,128)} fusion(bf16[1024,480]{0,1:T(8,128)(2,1)S(1)} %copy-done, bf16[480,8192]{1,0:T(8,128)(2,1)} %param.13), kind=kOutput, calls=%fused_computation.42 | convolution fusion | flops 8053063680 | bytes 42401792 | tf_op jit(solution)/shard_map/dot_general | solution.py:38
  27.0 0.0 copy-done.5
  27.0 2.3 add_dynamic-update-slice_fusion
  29.3 17.2 %convert_element_type.52 = bf16[1024,8192]{1,0:T(8,128)(2,1)} convert(f32[1024,8192]{1,0:T(8,128)} %add_dynamic-update-slice_fusion) | non-fusion elementwise | flops 8388608 | bytes 50331648 | tf_op jit(solution)/shard_map/convert_element_type | solution.py:43
  46.5 0.0 copy-start.6
  46.5 0.0 copy-start.10
  46.5 0.0 copy-start.11
  46.5 0.0 all-reduce.2.cloned.1.call-update
  46.5 0.7 copy-done.6
  47.3 0.5 copy-done.10
  47.8 0.0 copy-done.11
  47.8 0.0 copy-start.8
  47.8 0.0 copy-start.12
  47.8 0.0 copy-start.9
  47.8 0.0 copy-start.7
  47.8 0.5 fusion.8
  48.2 1.0 copy.17
  49.3 1.5 fusion.9
  50.8 1.8 copy.18
  52.6 0.0 copy-done.8
  52.6 0.0 copy-done.12
  52.6 0.0 copy-done.9
  52.6 0.0 copy-done.7
  52.6 4.2 %fusion.7 = bf16[8192,128]{1,0:T(8,128)(2,1)} fusion(bf16[64,128]{1,0:T(8,128)(2,1)S(1)} %copy-done.7, bf16[8192,128]{1,0:T(8,128)(2,1)} %param.15, s32[8192]{0:T(1024)S(1)} %copy-done.6), kind=kOutput, calls=%fused_computation.9 | convolution fusion | flops 137887744 | bytes 4243456 | tf_op jit(solution)/shard_map/dot_general | solution.py:8
  56.8 314.3 %all-reduce.2.cloned.1.call-done = bf16[1024,8192]{1,0:T(8,128)(2,1)} async-done(((bf16[1024,8192]{1,0:T(8,128)(2,1)}), bf16[1024,8192]{1,0:T(8,128)(2,1)}) %all-reduce.2.cloned.1.call-update) | async-done | bytes 16777232 | tf_op jit(solution)/shard_map/psum | solution.py:43
  371.1 0.0 copy-start.2
  371.1 0.0 copy-start.3
  371.1 8.2 %fusion = f32[1024]{0:T(1024)S(1)} fusion(bf16[1024,8192]{1,0:T(8,128)(2,1)} %all-reduce.2.cloned.1.call-done), kind=kLoop, calls=%fused_computation.2 | loop fusion | flops 25164800 | bytes 16781312 | tf_op jit(solution)/shard_map/reduce_sum | solution.py:46
  379.3 0.0 copy-done.2
  379.3 0.0 copy-done.3
  379.3 0.0 copy-start.1
  379.3 12.7 %fusion.3 = f32[1024,192]{0,1:T(8,128)S(1)} fusion(bf16[1024,8192]{1,0:T(8,128)(2,1)} %all-reduce.2.cloned.1.call-done, f32[8192]{0:T(1024)S(1)} %convert_element_type.54, f32[1024]{0:T(1024)S(1)} %add_rsqrt_fusion, bf16[8192,32]{1,0:T(8,128)(2,1)S(1)} %copy-done.2, bf16[8192,32]{1,0:T(8,128)(2,1)S(1)} %copy.17, bf16[8192,128]{1,0:T(8,128)(2,1)S(1)} %copy-done.3), kind=kOutput, calls=%fused_computation.5 | convolution fusion | flops 3264217088 | bytes 20746240 | tf_op jit(solution)/shard_map/dot_general | solution.py:47
  392.0 0.0 copy-start.4
  392.0 0.9 copy-done.4
  392.9 0.1 fusion.18
  393.0 0.8 copy.19
  393.9 1.0 fusion.21
  394.9 0.7 pad_maximum_fusion
  395.6 1.9 constant_dynamic-slice_fusion
  397.5 0.0 copy-done.1
  (4 shorter events, 0.0 us)
Async XLA Ops:
  7.2 1.2 copy-start
  7.2 363.9 %all-reduce.2.cloned.1.call-start = ((), (), s32[]{:S(2)}) async-start(), calls=%async_computation | async-start | bytes 33554432 | tf_op jit(solution)/shard_map/psum | solution.py:43
  8.4 18.6 %copy-start.5 = (bf16[32,8192]{1,0:T(8,128)(2,1)S(1)}, bf16[32,8192]{1,0:T(8,128)(2,1)}, u32[]{:S(2)}) copy-start(bf16[32,8192]{1,0:T(8,128)(2,1)} %param.12) | copy-start | bytes 1572868
  46.5 0.8 copy-start.6
  46.5 1.2 copy-start.10
  46.5 1.2 copy-start.11
  47.8 4.8 %copy-start.8 = (bf16[8192]{0:T(1024)(128)(2,1)S(1)}, bf16[8192]{0:T(1024)(128)(2,1)}, u32[]{:S(2)}) copy-start(bf16[8192]{0:T(1024)(128)(2,1)} %param.14) | copy-start | bytes 49156
  47.8 4.8 %copy-start.12 = (bf16[128]{0:T(256)(128)(2,1)S(1)}, bf16[128]{0:T(256)(128)(2,1)}, u32[]{:S(2)}) copy-start(bf16[128]{0:T(256)(128)(2,1)} %param.20) | copy-start | bytes 772
  47.8 4.8 %copy-start.9 = (bf16[2,32]{1,0:T(2,128)(2,1)S(1)}, bf16[2,32]{1,0:T(2,128)(2,1)}, u32[]{:S(2)}) copy-start(bf16[2,32]{1,0:T(2,128)(2,1)} %param.21) | copy-start | bytes 388
  47.8 4.8 %copy-start.7 = (bf16[64,128]{1,0:T(8,128)(2,1)S(1)}, bf16[64,128]{1,0:T(8,128)(2,1)}, u32[]{:S(2)}) copy-start(bf16[64,128]{1,0:T(8,128)(2,1)} %param.16) | copy-start | bytes 49156
  371.1 8.2 %copy-start.2 = (bf16[8192,32]{1,0:T(8,128)(2,1)S(1)}, bf16[8192,32]{1,0:T(8,128)(2,1)}, u32[]{:S(2)}) copy-start(bf16[8192,32]{1,0:T(8,128)(2,1)} %copy.18) | copy-start | bytes 1572868
  371.1 8.2 %copy-start.3 = (bf16[8192,128]{1,0:T(8,128)(2,1)S(1)}, bf16[8192,128]{1,0:T(8,128)(2,1)}, u32[]{:S(2)}) copy-start(bf16[8192,128]{1,0:T(8,128)(2,1)} %fusion.7) | copy-start | bytes 6291460
  379.3 18.1 %copy-start.1 = (bf16[1024,480]{0,1:T(8,128)(2,1)S(1)}, bf16[1024,480]{0,1:T(8,128)(2,1)}, u32[]{:S(2)}) copy-start(bf16[1024,480]{0,1:T(8,128)(2,1)} %param.11) | copy-start | bytes 2949124
  392.0 0.9 copy-start.4
Sparse Core Ops, SparseCore 0:
  46.7 324.3 all-reduce.1
where the time goes:
time: 406 us; the launch traced here: 404 us
  waiting for transfers between devices  314 us (77%)
  matrix products  37.4 us (9%)
  other arithmetic  29.6 us (7%)
  between operations  14.2 us (3%)
  local copies, waits for them, and re-layouts  8.79 us (2%)
    psum x1, waiting for transfers between devices, per_device(): summed = lax.psum(partial_value.astype(jnp.bfloat16), 'tensor')  314 us
    dot_general x1, matrix products, per_device(): jnp.dot(hidden, down_weight, preferred_element_type=jnp.float32)  18.6 us
    convert_element_type x1, other arithmetic, per_device(): summed = lax.psum(partial_value.astype(jnp.bfloat16), 'tensor')  17.2 us
    dot_general x1, matrix products, per_device(): jnp.dot((scaled * gain_wide).astype(jnp.bfloat16), joined, preferred_elem...  12.7 us
    reduce_sum x1, other arithmetic, per_device(): jnp.mean(widened * widened, axis=1, keepdims=True) + 1e-06  8.2 us
  transfers between devices with their start and end apart: 1, of which 1 were waited for; matrix products, arithmetic and copies ran while one was open for 2% of the time, Pallas kernels for 0%

commit v1 on v0

v1 whole, which is shorter than its diff:
```python
import functools

import jax
import jax.numpy as jnp
from jax import lax
from jax.experimental import pallas as pl
from jax.experimental.pallas import tpu as pltpu
from jax.sharding import PartitionSpec as P

MESH = pl.DeviceIdType.MESH
NX, NZ, NY, NC = 4, 8, 4, 2
F32, BF16 = jnp.float32, jnp.bfloat16
HALF = 1024
SUB = 512
AHEAD = 3


def kernel(
    hid, res, w, wq, bias, nr_out, q_out, kv_out,
    wb, hb, rsb, yb, wqb, part, snd, resb,
    l_h, l_w, l_r, l_q, l_n,
    h_s, h_r, w_s, w_r, wy_s, wy_r, wc_s, wc_r, q_s, q_r, qy_s, qy_r, qc_s, qc_r,
    r_s, r_r, rs_s, rs_r, ag_s, ag_r, n_s, n_r, p_s, p_r,
):
    t, d = lax.axis_index("tensor"), lax.axis_index("dp")
    x, z = t // NZ, t % NZ
    y, c = d // NC, d % NC

    def at(xx, zz, yy, cc):
        return {"tensor": xx * NZ + zz, "dp": yy * NC + cc}

    def to_x(o):
        return at((x + o) % NX, z, y, c)

    def to_z(o):
        return at(x, (z + o + NZ) % NZ, y, c)

    def to_y(o):
        return at(x, z, (y + o) % NY, c)

    sibling = at(x, z, y, 1 - c)

    def remote(src, dst, ss, rs, device):
        return pltpu.make_async_remote_copy(
            src_ref=src, dst_ref=dst, send_sem=ss, recv_sem=rs, device_id=device, device_id_type=MESH
        )

    def xs(o):
        return (x + o) % NX

    rank = c * NY + y
    def hid_local(u):
        zl, zh = (z + 2 * NZ - 1 - u) % NZ, (z + 1 + u) % NZ
        return (
            pltpu.make_async_copy(hid.at[pl.ds(0, 2), zl], hb.at[x, u, pl.ds(0, 2)], l_h.at[u, 0]),
            pltpu.make_async_copy(hid.at[pl.ds(2, 2), zh], hb.at[x, u, pl.ds(2, 2)], l_h.at[u, 1]),
        )

    def w_local(r):
        return pltpu.make_async_copy(w.at[:, pl.ds(x * 2 * HALF + r * HALF, HALF)], wb.at[r, x], l_w.at[r])

    def res_local():
        return pltpu.make_async_copy(res.at[:, pl.ds(x * 2 * HALF, 2 * HALF)], resb.at[x], l_r.at[0])

    def wq_local():
        return pltpu.make_async_copy(
            wq.at[x], wqb.at[:, pl.ds(rank * 128, 128), pl.ds(x * 256, 256)], l_q.at[0]
        )

    def nr_local(r):
        return pltpu.make_async_copy(
            yb.at[r, 0, x], nr_out.at[:, pl.ds(x * 2 * HALF + r * HALF, HALF)], l_n.at[r]
        )

    def h_direct(u, side):
        o = 1 if side == 0 else 3
        return remote(hb.at[x, u], hb.at[x, u], h_s.at[u, side], h_r.at[u, side], to_x(o))

    def h_direct_in(u, side):
        o = 3 if side == 0 else 1
        ref = hb.at[xs(o), u]
        return remote(ref, ref, h_s.at[u, side], h_r.at[u, side], to_x(o))

    def h_forward(u, side):
        src = xs(3) if side == 0 else xs(1)
        ref = hb.at[src, u, pl.ds(2 * side, 2)]
        return remote(ref, ref, h_s.at[u, 2 + side], h_r.at[u, 2 + side], to_x(1 if side == 0 else 3))

    def h_forward_in(u, side):
        ref = hb.at[xs(2), u, pl.ds(2 * side, 2)]
        return remote(ref, ref, h_s.at[u, 2 + side], h_r.at[u, 2 + side], to_x(2))

    def w_x(r, o):
        cols = pl.ds(xs(o) * 2 * HALF + r * HALF + rank * 128, 128)
        return remote(
            w.at[:, cols], wb.at[r, x, :, pl.ds(rank * 128, 128)], w_s.at[r, o - 1], w_r.at[r, o - 1], to_x(o)
        )

    def w_x_in(r, o):
        ref = wb.at[r, xs(NX - o), :, pl.ds(rank * 128, 128)]
        return remote(ref, ref, w_s.at[r, o - 1], w_r.at[r, o - 1], to_x(o))

    def w_y(r, o, p):
        ref = wb.at[r, xs(NX - o), :, pl.ds(rank * 128, 128)]
        return remote(ref, ref, wy_s.at[r, o - 1, p - 1], wy_r.at[r, o - 1, p - 1], to_y(p))

    def w_y_in(r, o, p):
        other = c * NY + (y + NY - p) % NY
        ref = wb.at[r, xs(NX - o), :, pl.ds(other * 128, 128)]
        return remote(ref, ref, wy_s.at[r, o - 1, p - 1], wy_r.at[r, o - 1, p - 1], to_y(p))

    def w_c(r, o):
        ref = wb.at[r, xs(NX - o), :, pl.ds(c * 512, 512)]
        return remote(ref, ref, wc_s.at[r, o - 1], wc_r.at[r, o - 1], sibling)

    def w_c_in(r, o):
        ref = wb.at[r, xs(NX - o), :, pl.ds((1 - c) * 512, 512)]
        return remote(ref, ref, wc_s.at[r, o - 1], wc_r.at[r, o - 1], sibling)

    def q_x(o):
        dst = wqb.at[:, pl.ds(rank * 128, 128), pl.ds(x * 256, 256)]
        return remote(wq.at[xs(o)], dst, q_s.at[o - 1], q_r.at[o - 1], to_x(o))

    def q_x_in(o):
        ref = wqb.at[:, pl.ds(rank * 128, 128), pl.ds(xs(NX - o) * 256, 256)]
        return remote(ref, ref, q_s.at[o - 1], q_r.at[o - 1], to_x(o))

    def q_y(p):
        ref = wqb.at[:, pl.ds(rank * 128, 128), :]
        return remote(ref, ref, qy_s.at[p - 1], qy_r.at[p - 1], to_y(p))

    def q_y_in(p):
        other = c * NY + (y + NY - p) % NY
        ref = wqb.at[:, pl.ds(other * 128, 128), :]
        return remote(ref, ref, qy_s.at[p - 1], qy_r.at[p - 1], to_y(p))

    def q_c():
        ref = wqb.at[:, pl.ds(c * 512, 512), :]
        return remote(ref, ref, qc_s.at[0], qc_r.at[0], sibling)

    def q_c_in():
        ref = wqb.at[:, pl.ds((1 - c) * 512, 512), :]
        return remote(ref, ref, qc_s.at[0], qc_r.at[0], sibling)

    def res_x(o):
        return remote(
            res.at[:, pl.ds(xs(o) * 2 * HALF, 2 * HALF)], resb.at[x], r_s.at[o - 1], r_r.at[o - 1], to_x(o)
        )

    def res_x_in(o):
        ref = resb.at[xs(NX - o)]
        return remote(ref, ref, r_s.at[o - 1], r_r.at[o - 1], to_x(o))

    def ring(buf, ss, rs, r, k, side, j):
        rows, cols = pl.ds(2 * side, 2), pl.ds(j * SUB, SUB)
        return remote(
            buf.at[r, k, rows, :, cols], buf.at[r, k + 1, rows, :, cols],
            ss.at[r, k, side, j], rs.at[r, k, side, j], to_z(1 if side == 0 else -1),
        )

    def ring_in(buf, ss, rs, r, k, side, j):
        rows, cols = pl.ds(2 * side, 2), pl.ds(j * SUB, SUB)
        ref = buf.at[r, k, rows, :, cols]
        return remote(ref, ref, ss.at[r, k - 1, side, j], rs.at[r, k - 1, side, j], to_z(1))

    def nr_x(r, o):
        return remote(
            yb.at[r, 0, xs(o)], nr_out.at[:, pl.ds(x * 2 * HALF + r * HALF, HALF)],
            n_s.at[r, o - 1], n_r.at[r, o - 1], to_x(o),
        )

    def nr_x_in(r, o):
        ref = nr_out.at[:, pl.ds(xs(NX - o) * 2 * HALF + r * HALF, HALF)]
        return remote(ref, ref, n_s.at[r, o - 1], n_r.at[r, o - 1], to_x(o))

    def part_x(k, o):
        return remote(snd.at[k, xs(o)], part.at[o - 1, k], p_s.at[k, o - 1], p_r.at[k, o - 1], to_x(o))

    def own_send(u):
        for copy in hid_local(u):
            copy.wait()
        for side in range(2):
            h_direct(u, side).start()

    def front(u):
        for side in range(2):
            h_direct_in(u, side).wait_recv()
            h_forward(u, side).start()

    def back(u):
        for side in range(2):
            h_forward_in(u, side).wait_recv()

    def w_spread_y(r):
        for o in (1, 3, 2):
            w_x_in(r, o).wait_recv()
            for p in (1, 3, 2):
                w_y(r, o, p).start()

    def w_spread_c(r):
        for o in (1, 3, 2):
            for p in (1, 3, 2):
                w_y_in(r, o, p).wait_recv()
            w_c(r, o).start()

    def w_ready(r):
        w_local(r).wait()
        for o in (1, 3, 2):
            w_c_in(r, o).wait_recv()

    def reduce_step(r, k):
        for j in range(2):
            cols = pl.ds(j * SUB, SUB)
            acc = jnp.zeros((128, SUB), F32)
            for xx in range(NX):
                acc += jnp.dot(
                    hb[xx, k].reshape(128, hb.shape[-1]), wb[r, xx, :, cols], preferred_element_type=F32
                )

            @pl.when(k > 0)
            def _():
                for side in range(2):
                    ring_in(rsb, rs_s, rs_r, r, k, side, j).wait_recv()

            acc += rsb[r, k, :, :, cols].reshape(128, SUB).astype(F32)

            @pl.when(k < NZ - 1)
            def _():
                rsb[r, k, :, :, cols] = acc.astype(BF16).reshape(4, 32, SUB)
                for side in range(2):
                    ring(rsb, rs_s, rs_r, r, k, side, j).start()

            @pl.when(k == NZ - 1)
            def _():
                own = resb[:, :, pl.ds(r * HALF + j * SUB, SUB)].reshape(128, SUB).astype(F32)
                yb[r, 0, :, :, cols] = (acc + own).astype(BF16).reshape(4, 32, SUB)

    def gather_step(r, k):
        for j in range(2):
            @pl.when(k > 0)
            def _():
                for side in range(2):
                    ring_in(yb, ag_s, ag_r, r, k, side, j).wait_recv()

            @pl.when(k < NZ - 1)
            def _():
                for side in range(2):
                    ring(yb, ag_s, ag_r, r, k, side, j).start()

    def residual_out(r):
        nr_local(r).start()
        for o in (1, 3, 2):
            nr_x(r, o).start()

    def project_step(k):
        acc = jnp.zeros((128, NX * 256), F32)
        squares = jnp.zeros((128, 1), F32)
        for r in range(2):
            rows = yb[r, k].reshape(128, HALF)
            acc += jnp.dot(rows, wqb[r], preferred_element_type=F32)
            wide = rows.astype(F32)
            squares += jnp.sum(wide * wide, axis=1, keepdims=True)
        high = squares.astype(BF16).astype(F32)
        low = squares - high
        lane = lax.broadcasted_iota(jnp.int32, (128, 256), 1)
        for xx in range(NX):
            piece = acc[:, xx * 256 : (xx + 1) * 256]
            piece = jnp.where(lane == 192, high, jnp.where(lane == 193, low, piece))
            snd[k, xx] = piece.astype(BF16)
        for o in (2, 1, 3):
            part_x(k, o).start()

    def combine_step(k):
        total = snd[k, x].astype(F32)
        for o in (1, 2, 3):
            part_x(k, o).wait_recv()
            total += part[o - 1, k].astype(F32)
        lane = lax.broadcasted_iota(jnp.int32, (128, 256), 1)
        squares = jnp.sum(jnp.where((lane == 192) | (lane == 193), total, 0.0), axis=1, keepdims=True)
        out = (total * lax.rsqrt(squares / (NX * 2 * HALF) + 1e-6) + bias[...]).astype(BF16)
        for side in range(2):
            zz = (z + NZ - k) % NZ if side == 0 else (z + k) % NZ
            for i in range(2):
                xt = 2 * side + i
                rows = out[xt * 32 : (xt + 1) * 32]
                q_out[xt, zz] = rows[:, :128]
                kv_out[0, xt, zz] = rows[:, 128:160]
                kv_out[1, xt, zz] = rows[:, 160:192]

    for u in range(NZ):
        for copy in hid_local(u):
            copy.start()
    for r in range(2):
        w_local(r).start()
    res_local().start()
    wq_local().start()
    rsb[0, 0] = jnp.zeros(rsb.shape[2:], BF16)
    rsb[1, 0] = jnp.zeros(rsb.shape[2:], BF16)

    barrier = pltpu.get_barrier_semaphore()
    friends = [to_x(1), to_x(2), to_x(3), to_z(1), to_z(-1), to_y(1), to_y(2), to_y(3), sibling]
    for friend in friends:
        pl.semaphore_signal(barrier, inc=1, device_id=friend, device_id_type=MESH)
    pl.semaphore_wait(barrier, len(friends))

    for o in (2, 1, 3):
        w_x(0, o).start()
    for u in range(3):
        own_send(u)
    w_spread_y(0)
    front(0)
    own_send(3)
    front(1)
    own_send(4)
    w_spread_c(0)
    front(2)
    own_send(5)
    w_ready(0)

    @pl.loop(0, NZ)
    def _(k):
        @pl.when(k + AHEAD < NZ)
        def _():
            front(k + AHEAD)

        @pl.when(k + 6 < NZ)
        def _():
            own_send(k + 6)

        @pl.when(k == 1)
        def _():
            for o in (2, 1, 3):
                w_x(1, o).start()

        @pl.when(k == 3)
        def _():
            w_spread_y(1)
            for o in (2, 1, 3):
                res_x(o).start()

        @pl.when(k == 4)
        def _():
            for o in (2, 1, 3):
                q_x(o).start()

        @pl.when(k == 6)
        def _():
            w_spread_c(1)

        @pl.when(k == 7)
        def _():
            res_local().wait()
            for o in (2, 1, 3):
                res_x_in(o).wait_recv()

        back(k)
        reduce_step(0, k)

    residual_out(0)
    w_ready(1)

    @pl.loop(0, NZ)
    def _(k):
        @pl.when(k == 0)
        def _():
            wq_local().wait()
            for o in (1, 3, 2):
                q_x_in(o).wait_recv()
            for p in (1, 3, 2):
                q_y(p).start()

        @pl.when(k == 5)
        def _():
            for p in (1, 3, 2):
                q_y_in(p).wait_recv()
            q_c().start()

        reduce_step(1, k)
        gather_step(0, k)

    residual_out(1)
    q_c_in().wait_recv()

    @pl.loop(0, NZ)
    def _(k):
        gather_step(1, k)
        project_step(k)

        @pl.when(k >= 3)
        def _():
            combine_step(k - 3)

    @pl.loop(NZ - 3, NZ)
    def _(k):
        combine_step(k)

    for r in range(2):
        nr_local(r).wait()
        for o in (1, 2, 3):
            nr_x_in(r, o).wait_recv()
            nr_x(r, o).wait_send()
            w_x(r, o).wait_send()
            w_c(r, o).wait_send()
            for p in (1, 2, 3):
                w_y(r, o, p).wait_send()
    for o in (1, 2, 3):
        q_x(o).wait_send()
        q_y(o).wait_send()
        res_x(o).wait_send()
    q_c().wait_send()

    @pl.loop(0, NZ)
    def _(k):
        for side in range(2):
            h_direct(k, side).wait_send()
            h_forward(k, side).wait_send()
        for o in (1, 2, 3):
            part_x(k, o).wait_send()

    @pl.loop(0, NZ - 1)
    def _(k):
        for r in range(2):
            for side in range(2):
                for j in range(2):
                    ring(rsb, rs_s, rs_r, r, k, side, j).wait_send()
                    ring(yb, ag_s, ag_r, r, k, side, j).wait_send()


def per_device(
    hidden,
    residual,
    down_weight,
    norm_gain,
    query_codes,
    query_scales,
    pair_codes,
    pair_scales,
    input_groups,
    query_bias,
    pair_bias,
):
    d = lax.axis_index("dp")
    rank = (d % NC) * NY + d // NC
    group_count = query_scales.shape[0]

    def share(a):
        return lax.dynamic_index_in_dim(a.reshape((NX, 2, 8, 128) + a.shape[1:]), rank, 2, keepdims=False)

    codes = jnp.concatenate([share(query_codes), share(pair_codes[0]), share(pair_codes[1])], axis=-1)
    scales = jnp.concatenate([query_scales, pair_scales[0], pair_scales[1]], axis=-1)
    selector = (share(input_groups)[..., None] == jnp.arange(group_count, dtype=jnp.int32)).astype(BF16)
    scale_rows = jnp.dot(selector.reshape(1024, group_count), scales, preferred_element_type=F32)
    scale_rows = scale_rows.reshape(codes.shape)
    gain = share(norm_gain).astype(F32)[..., None]
    wq = (codes.astype(F32) * scale_rows * gain).astype(BF16)
    wq = jnp.pad(wq, ((0, 0), (0, 0), (0, 0), (0, 64)))
    bias = jnp.concatenate([query_bias, pair_bias[0], pair_bias[1], jnp.zeros((64,), BF16)]).astype(F32)[None]
    depth = hidden.shape[1]
    dma = pltpu.SemaphoreType.DMA
    pairs = []
    for shape in (
        (8, 4), (2, 3), (2, 3, 3), (2, 3), (3,), (3,), (1,),
        (3,), (2, 7, 2, 2), (2, 7, 2, 2), (2, 3), (8, 3),
    ):
        pairs += [dma(shape), dma(shape)]
    new_residual, queries, key_values = pl.pallas_call(
        kernel,
        out_shape=(
            jax.ShapeDtypeStruct(residual.shape, BF16),
            jax.ShapeDtypeStruct((4, 8, 32, 128), BF16),
            jax.ShapeDtypeStruct((2, 4, 8, 32, 32), BF16),
        ),
        in_specs=[pl.BlockSpec(memory_space=pl.ANY)] * 4 + [pl.BlockSpec(memory_space=pltpu.VMEM)],
        out_specs=(
            pl.BlockSpec(memory_space=pl.ANY),
            pl.BlockSpec(memory_space=pltpu.VMEM),
            pl.BlockSpec(memory_space=pltpu.VMEM),
        ),
        scratch_shapes=[
            pltpu.VMEM((2, NX, depth, HALF), BF16),
            pltpu.VMEM((NX, NZ, 4, 32, depth), BF16),
            pltpu.VMEM((2, NZ, 4, 32, HALF), BF16),
            pltpu.VMEM((2, NZ, 4, 32, HALF), BF16),
            pltpu.VMEM((2, HALF, NX * 256), BF16),
            pltpu.VMEM((3, NZ, 128, 256), BF16),
            pltpu.VMEM((NZ, NX, 128, 256), BF16),
            pltpu.VMEM((4, 32, 2 * HALF), BF16),
            dma((8, 2)), dma((2,)), dma((1,)), dma((1,)), dma((2,)),
        ] + pairs,
        compiler_params=pltpu.CompilerParams(
            collective_id=0, has_side_effects=True, vmem_limit_bytes=58 * 2**20
        ),
        cost_estimate=pl.CostEstimate(flops=12_000_000_000, bytes_accessed=14_000_000, transcendentals=0),
    )(hidden.reshape(4, 8, 32, depth), residual, down_weight, wq, bias)
    return new_residual, queries.reshape(1024, 128), key_values.reshape(2, 1024, 32)


def solution(mesh):
    in_specs = (
        P("dp", "tensor"),
        P(("dp", "tensor"), None),
        P("tensor", None),
        P(),
        P(None, "tensor"),
        P(None, "tensor"),
        P(None, None, "tensor"),
        P(None, None, "tensor"),
        P(),
        P("tensor"),
        P(None, "tensor"),
    )
    out_specs = (P(("dp", "tensor"), None), P("dp", "tensor"), P(None, "dp", "tensor"))
    return jax.shard_map(
        per_device, mesh=mesh, in_specs=in_specs, out_specs=out_specs, check_vma=False
    )
```

time: 406 us -> 173 us (0.43)
  waiting for transfers between devices: 314 us -> 0 us
  Pallas kernels: 0 us -> 157 us
  matrix products: 37.4 us -> 1.55 us
  other arithmetic: 29.6 us -> 1.37 us
  between operations: 14.2 us -> 0.76 us
    psum x1 -> x0, waiting for transfers between devices: 314 us -> none  [per_device(): summed = lax.psum(partial_value.astype(jnp.bfloat16), 'tensor')]
    pallas_call x0 -> x1, Pallas kernels: none -> 157 us  [per_device(): pl.pallas_call(kernel, out_shape=(jax.ShapeDtypeStruct(residual.shape, BF...]
    dot_general x5 -> x1, matrix products: 37.4 us -> 1.55 us  [per_device(): jnp.dot(selector.reshape(1024, group_count), scales, preferred_element_ty...]
    convert_element_type x4 -> x2, other arithmetic: 17.3 us -> 1.37 us  [the longest x1 0.73 us: per_device(): gain = share(norm_gain).astype(F32)[..., None]]
    reduce_sum x1 -> x0, other arithmetic: 8.2 us -> none  [per_device(): jnp.mean(widened * widened, axis=1, keepdims=True) + 1e-06]
    unnamed x27 -> x23, local copies, waits for them, and re-layouts: 4.13 us -> 10.3 us
  transfers between devices with their start and end apart: 1 -> 0, of which waited for: 1 -> 0; matrix products, arithmetic and copies ran while one was open for 2% -> 0% of each run, Pallas kernels for 0% -> 0%
where the time goes in v1:
time: 173 us
  Pallas kernels  157 us (91%)
  local copies, waits for them, and re-layouts  12.3 us (7%)
    pallas_call x1, Pallas kernels, per_device(): pl.pallas_call(kernel, out_shape=(jax.ShapeDtypeStruct(residual.shape, BF...  157 us
    unnamed x23, local copies, waits for them, and re-layouts  10.3 us

profile of v1, /device:TPU:8, one launch (start us, length us, event | category | flops | bytes accessed | tf_op | source)
XLA Modules:
  0.0 173.1 jit_solution(9840093736219081196)
XLA Ops:
  0.6 0.0 copy-start
  0.7 1.4 slice_bitcast_fusion.1
  2.1 0.0 copy-start.2
  2.1 0.0 copy-start.5
  2.1 0.1 copy.37
  2.2 0.1 copy.38
  2.4 0.3 constant_dynamic-slice_fusion.1
  2.7 0.9 copy.33
  3.5 0.0 copy-start.3
  3.5 0.0 copy-start.4
  3.5 0.0 copy-start.1
  3.5 0.9 copy.34
  4.4 0.0 copy-done
  4.4 0.7 dynamic-slice_convert_fusion
  5.1 0.8 constant_dynamic-slice_fusion
  5.9 0.0 copy-done.2
  5.9 0.1 copy.35
  6.0 0.1 copy.36
  6.1 0.0 copy-done.5
  6.1 1.6 fusion.1
  7.7 0.9 pad.4.wq
  8.6 0.0 copy-done.3
  8.6 0.1 pad.8.clone
  8.7 0.0 copy-done.4
  8.7 0.6 fusion.7.bias
  9.3 0.0 copy-done.1
  9.3 1.3 copy.22
  10.6 157.0 %shard_map.130 = (bf16[32,8192]{1,0:T(8,128)(2,1)}, bf16[4,8,32,128]{3,2,1,0:T(8,128)(2,1)}, bf16[2,4,8,32,32]{4,3,2,1,0:T(8,128)(2,1)}) custom-call(bf16[4,8,32,480]{3,2,1,0:T(8,128)(2,1)} %bitcast.37, bf16[32,8192]{1,0:T(8,128)(2,1)} %res.1, bf16[480,8192]{1,0:T(8,128)(2,1)} %w.1, bf16[4,2,128,256]{3,2,1,0:T(8,128)(2,1)} %pad.4.wq, f32[1,256]{1,0:T(1,128)} %fusion.7.bias), custom_call_target="tpu_custom_call" | custom-call | flops 12000000000 | bytes 14000000 | tf_op jit(solution)/shard_map/pallas_call | solution.py:466
  167.6 1.9 %copy.29 = bf16[2,1024,32]{1,2,0:T(8,128)(2,1)} copy(bf16[2,1024,32]{2,1,0:T(8,128)(2,1)} %bitcast.40) | data formatting | bytes 262144
  169.5 1.9 %copy.41 = bf16[32,8192]{1,0:T(8,128)(2,1)} copy(bf16[32,8192]{1,0:T(8,128)(2,1)} %get-tuple-element.26) | data formatting | bytes 1048576
  171.4 1.7 copy.42
  (4 shorter events, 0.0 us)
Async XLA Ops:
  0.6 3.8 %copy-start = (bf16[8192,128]{1,0:T(8,128)(2,1)S(1)}, bf16[8192,128]{1,0:T(8,128)(2,1)}, u32[]{:S(2)}) copy-start(bf16[8192,128]{1,0:T(8,128)(2,1)} %param.15) | copy-start | bytes 6291460
  2.1 3.8 %copy-start.2 = (bf16[2,64,32]{1,2,0:T(8,128)(2,1)S(1)}, bf16[2,64,32]{1,2,0:T(8,128)(2,1)}, u32[]{:S(2)}) copy-start(bf16[2,64,32]{1,2,0:T(8,128)(2,1)} %param.18) | copy-start | bytes 24580
  2.1 4.0 %copy-start.5 = (bf16[64,128]{1,0:T(8,128)(2,1)S(1)}, bf16[64,128]{1,0:T(8,128)(2,1)}, u32[]{:S(2)}) copy-start(bf16[64,128]{1,0:T(8,128)(2,1)} %param.16) | copy-start | bytes 49156
  3.5 5.1 %copy-start.3 = (bf16[2,32]{1,0:T(2,128)(2,1)S(1)}, bf16[2,32]{1,0:T(2,128)(2,1)}, u32[]{:S(2)}) copy-start(bf16[2,32]{1,0:T(2,128)(2,1)} %param.21) | copy-start | bytes 388
  3.5 5.1 %copy-start.4 = (bf16[128]{0:T(256)(128)(2,1)S(1)}, bf16[128]{0:T(256)(128)(2,1)}, u32[]{:S(2)}) copy-start(bf16[128]{0:T(256)(128)(2,1)} %param.20) | copy-start | bytes 772
  3.5 5.8 %copy-start.1 = (bf16[1024,480]{0,1:T(8,128)(2,1)S(1)}, bf16[1024,480]{0,1:T(8,128)(2,1)}, u32[]{:S(2)}) copy-start(bf16[1024,480]{0,1:T(8,128)(2,1)} %param.11) | copy-start | bytes 2949124

commit v2 on v0

v2 whole, which is shorter than its diff:
```python
import jax
import jax.numpy as jnp
from jax import lax
from jax.experimental import pallas as pl
from jax.experimental.pallas import tpu as pltpu
from jax.sharding import PartitionSpec as P

MESH = pl.DeviceIdType.MESH
NX, NZ, NY, NC = 4, 8, 4, 2
F32, BF16 = jnp.float32, jnp.bfloat16
NQ, QW = 4, 512
XW = NQ * QW


def kernel(
    hid, res, w, wq, bias, nr_out, q_out, kv_out,
    wb, hb, rsb, yb, wqp, kvw, part, snd, resb,
    l_h, l_w, l_r, l_q, l_n,
    h_s, h_r, w_s, w_r, wy_s, wy_r, wc_s, wc_r, q_s, q_r, qy_s, qy_r, qc_s, qc_r,
    r_s, r_r, rs_s, rs_r, ag_s, ag_r, n_s, n_r, p_s, p_r,
):
    t, d = lax.axis_index("tensor"), lax.axis_index("dp")
    x, z = t // NZ, t % NZ
    y, c = d // NC, d % NC
    depth = hid.shape[-1]
    half = depth // 2
    cut = half // 32 * 16 + 16

    def at(xx, zz, yy, cc):
        return {"tensor": xx * NZ + zz, "dp": yy * NC + cc}

    def to_x(o):
        return at((x + o) % NX, z, y, c)

    def to_z(o):
        return at(x, (z + o + NZ) % NZ, y, c)

    def to_y(o):
        return at(x, z, (y + o) % NY, c)

    sibling = at(x, z, y, 1 - c)

    def remote(src, dst, ss, rs, device):
        return pltpu.make_async_remote_copy(
            src_ref=src, dst_ref=dst, send_sem=ss, recv_sem=rs, device_id=device, device_id_type=MESH
        )

    def xs(o):
        return (x + o) % NX

    def ys(o):
        return (y + o) % NY

    step_of = (1, 3)

    def hid_local(u):
        zl, zh = (z + 2 * NZ - 1 - u) % NZ, (z + 1 + u) % NZ
        return (
            pltpu.make_async_copy(hid.at[pl.ds(0, 2), zl], hb.at[0, u, pl.ds(0, 2)], l_h.at[u, 0]),
            pltpu.make_async_copy(hid.at[pl.ds(2, 2), zh], hb.at[0, u, pl.ds(2, 2)], l_h.at[u, 1]),
        )

    def w_local(q, i):
        return pltpu.make_async_copy(
            w.at[:, pl.ds(x * XW + q * QW + i * 128, 128)], wb.at[q, 0, i], l_w.at[q, i]
        )

    def res_local():
        return pltpu.make_async_copy(res.at[:, pl.ds(x * XW, XW)], resb.at[x], l_r.at[0])

    rank = c * NY + y

    def wq_local():
        return pltpu.make_async_copy(wq.at[x], wqp.at[0, rank], l_q.at[0])

    def nr_local(q):
        return pltpu.make_async_copy(
            yb.at[q, 0, x], nr_out.at[:, pl.ds(x * XW + q * QW, QW)], l_n.at[q]
        )

    def h_direct(u, side):
        return remote(
            hb.at[0, u], hb.at[NX - step_of[side], u], h_s.at[u, side], h_r.at[u, side], to_x(step_of[side])
        )

    def h_direct_in(u, side):
        ref = hb.at[NX - step_of[side], u]
        return remote(ref, ref, h_s.at[u, side], h_r.at[u, side], to_x(step_of[side]))

    def h_forward(u, side):
        rows = pl.ds(2 * side, 2)
        return remote(
            hb.at[NX - step_of[side], u, rows], hb.at[2, u, rows],
            h_s.at[u, 2 + side], h_r.at[u, 2 + side], to_x(step_of[side]),
        )

    def h_forward_in(u, side):
        ref = hb.at[2, u, pl.ds(2 * side, 2)]
        return remote(ref, ref, h_s.at[u, 2 + side], h_r.at[u, 2 + side], to_x(step_of[side]))

    def w_x(q, o):
        cols = pl.ds(xs(o) * XW + q * QW + y * 128, 128)
        rows = pl.ds(c * half, half)
        return remote(
            w.at[rows, cols], wb.at[q, NX - o, y, rows], w_s.at[q, o - 1], w_r.at[q, o - 1], to_x(o)
        )

    def w_x_in(q, o):
        ref = wb.at[q, NX - o, y, pl.ds(c * half, half)]
        return remote(ref, ref, w_s.at[q, o - 1], w_r.at[q, o - 1], to_x(o))

    def w_y(q, side):
        ref = wb.at[q, pl.ds(1, NX - 1), y, pl.ds(c * half, half)]
        return remote(ref, ref, wy_s.at[q, side], wy_r.at[q, side], to_y(step_of[side]))

    def w_y_in(q, side):
        ref = wb.at[q, pl.ds(1, NX - 1), ys(NY - step_of[side]), pl.ds(c * half, half)]
        return remote(ref, ref, wy_s.at[q, side], wy_r.at[q, side], to_y(step_of[side]))

    def w_part(q, yy, side):
        rows = pl.ds(c * half, cut) if side == 0 else pl.ds(c * half + cut, half - cut)
        return wb.at[q, pl.ds(1, NX - 1), yy, rows]

    def w_forward(q, side):
        ref = w_part(q, ys(NY - step_of[side]), side)
        return remote(ref, ref, wy_s.at[q, 2 + side], wy_r.at[q, 2 + side], to_y(step_of[side]))

    def w_forward_in(q, side):
        ref = w_part(q, ys(2), side)
        return remote(ref, ref, wy_s.at[q, 2 + side], wy_r.at[q, 2 + side], to_y(step_of[side]))

    def w_c(q):
        ref = wb.at[q, pl.ds(1, NX - 1), :, pl.ds(c * half, half)]
        return remote(ref, ref, wc_s.at[q], wc_r.at[q], sibling)

    def w_c_in(q):
        ref = wb.at[q, pl.ds(1, NX - 1), :, pl.ds((1 - c) * half, half)]
        return remote(ref, ref, wc_s.at[q], wc_r.at[q], sibling)

    def q_x(o):
        return remote(wq.at[xs(o)], wqp.at[NX - o, rank], q_s.at[o - 1], q_r.at[o - 1], to_x(o))

    def q_x_in(o):
        ref = wqp.at[NX - o, rank]
        return remote(ref, ref, q_s.at[o - 1], q_r.at[o - 1], to_x(o))

    def q_y(side):
        ref = wqp.at[:, rank]
        return remote(ref, ref, qy_s.at[side], qy_r.at[side], to_y(step_of[side]))

    def q_y_in(side):
        ref = wqp.at[:, c * NY + ys(NY - step_of[side])]
        return remote(ref, ref, qy_s.at[side], qy_r.at[side], to_y(step_of[side]))

    def q_forward(side):
        ref = wqp.at[:, c * NY + ys(NY - step_of[side]), pl.ds(192 * side, 192)]
        return remote(ref, ref, qy_s.at[2 + side], qy_r.at[2 + side], to_y(step_of[side]))

    def q_forward_in(side):
        ref = wqp.at[:, c * NY + ys(2), pl.ds(192 * side, 192)]
        return remote(ref, ref, qy_s.at[2 + side], qy_r.at[2 + side], to_y(step_of[side]))

    def q_c():
        ref = wqp.at[:, pl.ds(c * NY, NY)]
        return remote(ref, ref, qc_s.at[0], qc_r.at[0], sibling)

    def q_c_in():
        ref = wqp.at[:, pl.ds((1 - c) * NY, NY)]
        return remote(ref, ref, qc_s.at[0], qc_r.at[0], sibling)

    def res_x(o):
        return remote(
            res.at[:, pl.ds(xs(o) * XW, XW)], resb.at[x], r_s.at[o - 1], r_r.at[o - 1], to_x(o)
        )

    def res_x_in(o):
        ref = resb.at[xs(NX - o)]
        return remote(ref, ref, r_s.at[o - 1], r_r.at[o - 1], to_x(o))

    def ring(buf, ss, rs, q, k, side):
        rows = pl.ds(2 * side, 2)
        return remote(
            buf.at[q, k, rows], buf.at[q, k + 1, rows],
            ss.at[q, k, side], rs.at[q, k, side], to_z(1 if side == 0 else -1),
        )

    def ring_in(buf, ss, rs, q, k, side):
        ref = buf.at[q, k, pl.ds(2 * side, 2)]
        return remote(ref, ref, ss.at[q, k - 1, side], rs.at[q, k - 1, side], to_z(1))

    def nr_x(q, o):
        return remote(
            yb.at[q, 0, xs(o)], nr_out.at[:, pl.ds(x * XW + q * QW, QW)],
            n_s.at[q, o - 1], n_r.at[q, o - 1], to_x(o),
        )

    def nr_x_in(q, o):
        ref = nr_out.at[:, pl.ds(xs(NX - o) * XW + q * QW, QW)]
        return remote(ref, ref, n_s.at[q, o - 1], n_r.at[q, o - 1], to_x(o))

    def part_x(k, o):
        return remote(snd.at[k, o], part.at[o - 1, k], p_s.at[k, o - 1], p_r.at[k, o - 1], to_x(o))

    others = (2, 1, 3)

    def h_send(u):
        for copy in hid_local(u):
            copy.wait()
        for side in range(2):
            h_direct(u, side).start()

    def h_pass(u):
        for side in range(2):
            h_direct_in(u, side).wait_recv()
            h_forward(u, side).start()

    def h_ready(u):
        for side in range(2):
            h_forward_in(u, side).wait_recv()

    def w_send(q):
        for o in others:
            w_x(q, o).start()

    def w_spread(q):
        for o in (1, 3, 2):
            w_x_in(q, o).wait_recv()
        for side in range(2):
            w_y(q, side).start()

    def w_pass(q):
        for side in range(2):
            w_y_in(q, side).wait_recv()
            w_forward(q, side).start()

    def w_share(q):
        for side in range(2):
            w_forward_in(q, side).wait_recv()
        w_c(q).start()

    def w_ready(q):
        for i in range(4):
            w_local(q, i).wait()
        w_c_in(q).wait_recv()

    def reduce_step(q, k):
        acc = jnp.zeros((128, QW), F32)
        for o in range(NX):
            weight = jnp.concatenate([wb[q, o, i] for i in range(4)], axis=1)
            acc += jnp.dot(hb[o, k].reshape(128, depth), weight, preferred_element_type=F32)

        @pl.when(k > 0)
        def _():
            for side in range(2):
                ring_in(rsb, rs_s, rs_r, q, k, side).wait_recv()

        acc += rsb[q, k].reshape(128, QW).astype(F32)

        @pl.when(k < NZ - 1)
        def _():
            rsb[q, k] = acc.astype(BF16).reshape(4, 32, QW)
            for side in range(2):
                ring(rsb, rs_s, rs_r, q, k, side).start()

        @pl.when(k == NZ - 1)
        def _():
            own = resb[:, :, pl.ds(pl.multiple_of(q * QW, QW), QW)].reshape(128, QW).astype(F32)
            yb[q, 0] = (acc + own).astype(BF16).reshape(4, 32, QW)
            for side in range(2):
                ring(yb, ag_s, ag_r, q, 0, side).start()
            nr_local(q).start()
            for o in others:
                nr_x(q, o).start()

    def gather_step(q, k):
        for side in range(2):
            ring_in(yb, ag_s, ag_r, q, k, side).wait_recv()

        @pl.when(k < NZ - 1)
        def _():
            for side in range(2):
                ring(yb, ag_s, ag_r, q, k, side).start()

    def project_step(k):
        acc_q = [jnp.zeros((128, 256), F32), jnp.zeros((128, 256), F32)]
        acc_kv = jnp.zeros((128, 256), F32)
        squares = jnp.zeros((128, 1), F32)
        for q in range(NQ):
            rows = yb[q, k].reshape(128, QW)
            for pair in range(2):
                weight = jnp.concatenate(
                    [
                        jnp.concatenate([wqp[2 * pair + i, 2 * q + j, 0:256] for j in range(2)], axis=0)
                        for i in range(2)
                    ],
                    axis=1,
                )
                acc_q[pair] += jnp.dot(rows, weight, preferred_element_type=F32)
            acc_kv += jnp.dot(rows, kvw[q * QW : (q + 1) * QW], preferred_element_type=F32)
            wide = rows.astype(F32)
            squares += jnp.sum(wide * wide, axis=1, keepdims=True)
        high = squares.astype(BF16).astype(F32)
        low = squares - high
        lane = lax.broadcasted_iota(jnp.int32, (128, 64), 1)
        extra = jnp.where(lane == 0, high, jnp.where(lane == 1, low, 0.0))
        for o in range(NX):
            snd[k, o, :, 0:128] = acc_q[o // 2][:, (o % 2) * 128 : (o % 2 + 1) * 128].astype(BF16)
            snd[k, o, :, 128:256] = jnp.concatenate(
                [acc_kv[:, o * 64 : (o + 1) * 64], extra], axis=1
            ).astype(BF16)
        for o in others:
            part_x(k, o).start()

    def combine_step(k):
        total = snd[k, 0].astype(F32)
        for o in (1, 2, 3):
            part_x(k, o).wait_recv()
            total += part[o - 1, k].astype(F32)
        lane = lax.broadcasted_iota(jnp.int32, (128, 256), 1)
        squares = jnp.sum(jnp.where((lane == 192) | (lane == 193), total, 0.0), axis=1, keepdims=True)
        out = (total * lax.rsqrt(squares / (NX * XW) + 1e-6) + bias[...]).astype(BF16)
        for side in range(2):
            zz = (z + NZ - k) % NZ if side == 0 else (z + k) % NZ
            for i in range(2):
                xt = 2 * side + i
                rows = out[xt * 32 : (xt + 1) * 32]
                q_out[xt, zz] = rows[:, :128]
                kv_out[0, xt, zz] = rows[:, 128:160]
                kv_out[1, xt, zz] = rows[:, 160:192]

    for u in range(NZ):
        for copy in hid_local(u):
            copy.start()
    for q in range(NQ):
        for i in range(4):
            w_local(q, i).start()
    res_local().start()
    wq_local().start()
    for q in range(NQ):
        rsb[q, 0] = jnp.zeros(rsb.shape[2:], BF16)

    barrier = pltpu.get_barrier_semaphore()
    friends = [to_x(1), to_x(2), to_x(3), to_z(1), to_z(-1), to_y(1), to_y(3), sibling]
    for friend in friends:
        pl.semaphore_signal(barrier, inc=1, device_id=friend, device_id_type=MESH)
    pl.semaphore_wait(barrier, len(friends))

    w_send(0)
    h_send(0)
    w_spread(0)
    w_send(1)
    w_send(2)
    h_pass(0)
    h_send(1)
    w_pass(0)
    w_spread(1)
    w_send(3)
    w_spread(2)
    w_share(0)
    h_pass(1)
    h_send(2)
    w_ready(0)
    w_pass(1)
    w_spread(3)

    @pl.loop(0, NZ)
    def _(s):
        h_ready(s)

        @pl.when(s == NZ - 1)
        def _():
            res_local().wait()
            for o in others:
                res_x_in(o).wait_recv()

        @pl.loop(0, NQ)
        def _(q):
            @pl.when((q == s) & (s > 0))
            def _():
                w_share(q)
                w_ready(q)

            @pl.when(q <= s)
            def _():
                reduce_step(q, jnp.where(s > 2 * q, s, jnp.maximum(2 * (s - q) - 1, 0)))

        @pl.loop(1, NQ)
        def _(q):
            @pl.when((q < s) & (s <= 2 * q))
            def _():
                reduce_step(q, 2 * (s - q))

        @pl.when(s < NQ - 2)
        def _():
            w_pass(s + 2)

        @pl.when(s < NZ - 2)
        def _():
            h_pass(s + 2)

        @pl.when(s < NZ - 3)
        def _():
            h_send(s + 3)

        @pl.when(s == 3)
        def _():
            for o in others:
                q_x(o).start()

        @pl.when(s == 4)
        def _():
            for o in others:
                res_x(o).start()
            wq_local().wait()
            for o in (1, 3, 2):
                q_x_in(o).wait_recv()
            for side in range(2):
                q_y(side).start()

        @pl.when(s == 5)
        def _():
            for side in range(2):
                q_y_in(side).wait_recv()
                q_forward(side).start()

        @pl.when(s == 6)
        def _():
            for side in range(2):
                q_forward_in(side).wait_recv()
            q_c().start()

    q_c_in().wait_recv()
    for i in range(2 * NY):
        packed = [wqp[o, i, 256:384] for o in range(NX)]
        for j in range(2):
            kvw[i * 256 + j * 128 : i * 256 + (j + 1) * 128] = jnp.concatenate(
                [p[:, j * 64 : (j + 1) * 64] for p in packed], axis=1
            )

    @pl.loop(0, NZ)
    def _(k):
        @pl.when(k > 0)
        def _():
            @pl.loop(0, NQ)
            def _(q):
                gather_step(q, k)

        project_step(k)

        @pl.when(k >= 2)
        def _():
            combine_step(k - 2)

    @pl.loop(NZ - 2, NZ)
    def _(k):
        combine_step(k)

    @pl.loop(0, NQ)
    def _(q):
        nr_local(q).wait()
        for o in (1, 2, 3):
            nr_x_in(q, o).wait_recv()
            nr_x(q, o).wait_send()
            w_x(q, o).wait_send()
        for side in range(2):
            w_y(q, side).wait_send()
            w_forward(q, side).wait_send()
        w_c(q).wait_send()

    for o in (1, 2, 3):
        q_x(o).wait_send()
        res_x(o).wait_send()
    for side in range(2):
        q_y(side).wait_send()
        q_forward(side).wait_send()
    q_c().wait_send()

    @pl.loop(0, NZ)
    def _(k):
        for side in range(2):
            h_direct(k, side).wait_send()
            h_forward(k, side).wait_send()
        for o in (1, 2, 3):
            part_x(k, o).wait_send()

    @pl.loop(0, NZ - 1)
    def _(k):
        for q in range(NQ):
            for side in range(2):
                ring(rsb, rs_s, rs_r, q, k, side).wait_send()
                ring(yb, ag_s, ag_r, q, k, side).wait_send()


def per_device(
    hidden,
    residual,
    down_weight,
    norm_gain,
    query_codes,
    query_scales,
    pair_codes,
    pair_scales,
    input_groups,
    query_bias,
    pair_bias,
):
    d = lax.axis_index("dp")
    rank = (d % NC) * NY + d // NC
    group_count = query_scales.shape[0]

    def share(a):
        return lax.dynamic_index_in_dim(a.reshape((NX, 8, 256) + a.shape[1:]), rank, 1, keepdims=False)

    codes = jnp.concatenate([share(query_codes), share(pair_codes[0]), share(pair_codes[1])], axis=-1)
    scales = jnp.concatenate([query_scales, pair_scales[0], pair_scales[1]], axis=-1)
    selector = (share(input_groups)[..., None] == jnp.arange(group_count, dtype=jnp.int32)).astype(BF16)
    scale_rows = jnp.dot(selector.reshape(1024, group_count), scales, preferred_element_type=F32)
    scale_rows = scale_rows.reshape(codes.shape)
    gain = share(norm_gain).astype(F32)[..., None]
    wq = (codes.astype(F32) * scale_rows * gain).astype(BF16)
    kv = jnp.concatenate([wq[:, :128, 128:], wq[:, 128:, 128:]], axis=-1)
    wq = jnp.concatenate([wq[:, :, :128], kv], axis=1)
    bias = jnp.concatenate([query_bias, pair_bias[0], pair_bias[1], jnp.zeros((64,), BF16)]).astype(F32)[None]
    depth = hidden.shape[1]
    dma = pltpu.SemaphoreType.DMA
    pairs = []
    for shape in (
        (8, 4), (NQ, 3), (NQ, 4), (NQ,), (3,), (4,), (1,),
        (3,), (NQ, 7, 2), (NQ, 7, 2), (NQ, 3), (8, 3),
    ):
        pairs += [dma(shape), dma(shape)]
    new_residual, queries, key_values = pl.pallas_call(
        kernel,
        out_shape=(
            jax.ShapeDtypeStruct(residual.shape, BF16),
            jax.ShapeDtypeStruct((4, 8, 32, 128), BF16),
            jax.ShapeDtypeStruct((2, 4, 8, 32, 32), BF16),
        ),
        in_specs=[pl.BlockSpec(memory_space=pl.ANY)] * 4 + [pl.BlockSpec(memory_space=pltpu.VMEM)],
        out_specs=(
            pl.BlockSpec(memory_space=pl.ANY),
            pl.BlockSpec(memory_space=pltpu.VMEM),
            pl.BlockSpec(memory_space=pltpu.VMEM),
        ),
        scratch_shapes=[
            pltpu.VMEM((NQ, NX, 4, depth, 128), BF16),
            pltpu.VMEM((NX, NZ, 4, 32, depth), BF16),
            pltpu.VMEM((NQ, NZ, 4, 32, QW), BF16),
            pltpu.VMEM((NQ, NZ, 4, 32, QW), BF16),
            pltpu.VMEM((NX, 8, 384, 128), BF16),
            pltpu.VMEM((XW, 256), BF16),
            pltpu.VMEM((3, NZ, 128, 256), BF16),
            pltpu.VMEM((NZ, NX, 128, 256), BF16),
            pltpu.VMEM((4, 32, XW), BF16),
            dma((8, 2)), dma((NQ, 4)), dma((1,)), dma((1,)), dma((NQ,)),
        ] + pairs,
        compiler_params=pltpu.CompilerParams(
            collective_id=0, has_side_effects=True, vmem_limit_bytes=58 * 2**20
        ),
        cost_estimate=pl.CostEstimate(flops=12_000_000_000, bytes_accessed=14_000_000, transcendentals=0),
    )(hidden.reshape(4, 8, 32, depth), residual, down_weight, wq, bias)
    return new_residual, queries.reshape(1024, 128), key_values.reshape(2, 1024, 32)


def solution(mesh):
    in_specs = (
        P("dp", "tensor"),
        P(("dp", "tensor"), None),
        P("tensor", None),
        P(),
        P(None, "tensor"),
        P(None, "tensor"),
        P(None, None, "tensor"),
        P(None, None, "tensor"),
        P(),
        P("tensor"),
        P(None, "tensor"),
    )
    out_specs = (P(("dp", "tensor"), None), P("dp", "tensor"), P(None, "dp", "tensor"))
    return jax.shard_map(
        per_device, mesh=mesh, in_specs=in_specs, out_specs=out_specs, check_vma=False
    )
```

time: 406 us -> 148 us (0.36)
  waiting for transfers between devices: 314 us -> 0 us
  Pallas kernels: 0 us -> 132 us
  matrix products: 37.4 us -> 1.55 us
  other arithmetic: 29.6 us -> 1.51 us
  between operations: 14.2 us -> 0.88 us
    psum x1 -> x0, waiting for transfers between devices: 314 us -> none  [per_device(): summed = lax.psum(partial_value.astype(jnp.bfloat16), 'tensor')]
    pallas_call x0 -> x1, Pallas kernels: none -> 132 us  [per_device(): pl.pallas_call(kernel, out_shape=(jax.ShapeDtypeStruct(residual.shape, BF...]
    dot_general x5 -> x1, matrix products: 37.4 us -> 1.55 us  [per_device(): jnp.dot(selector.reshape(1024, group_count), scales, preferred_element_ty...]
    convert_element_type x4 -> x2, other arithmetic: 17.3 us -> 0.65 us  [the longest x1 0.64 us: per_device(): jnp.concatenate([query_bias, pair_bias[0], pair_bias[1], jnp.zeros((64,),...]
    reduce_sum x1 -> x0, other arithmetic: 8.2 us -> none  [per_device(): jnp.mean(widened * widened, axis=1, keepdims=True) + 1e-06]
    unnamed x27 -> x28, local copies, waits for them, and re-layouts: 4.13 us -> 8.96 us
  transfers between devices with their start and end apart: 1 -> 0, of which waited for: 1 -> 0; matrix products, arithmetic and copies ran while one was open for 2% -> 0% of each run, Pallas kernels for 0% -> 0%
where the time goes in v2:
time: 148 us; the launch traced here: 147 us
  Pallas kernels  132 us (89%)
  local copies, waits for them, and re-layouts  10.9 us (7%)
  matrix products  1.55 us (1%)
  other arithmetic  1.51 us (1%)
    pallas_call x1, Pallas kernels, per_device(): pl.pallas_call(kernel, out_shape=(jax.ShapeDtypeStruct(residual.shape, BF...  132 us
    unnamed x28, local copies, waits for them, and re-layouts  8.96 us

profile of v2, /device:TPU:8, one launch (start us, length us, event | category | flops | bytes accessed | tf_op | source)
XLA Modules:
  0.0 147.3 jit_solution(7248420766290787296)
XLA Ops:
  0.6 0.0 copy-start
  0.7 1.4 fusion.9
  2.1 0.0 copy-start.2
  2.1 0.0 copy-start.3
  2.1 0.0 copy-start.4
  2.1 0.0 copy-start.7
  2.1 0.1 copy.38
  2.3 0.1 copy.39
  2.4 0.3 constant_dynamic-slice_fusion.1
  2.7 0.9 copy.34
  3.5 0.9 copy.35
  4.4 0.0 copy-done
  4.4 0.0 copy-done.2
  4.5 0.0 copy-start.5
  4.5 0.0 copy-start.6
  4.5 0.0 copy-start.1
  4.5 0.0 copy-done.3
  4.6 0.0 copy-done.4
  4.6 0.1 copy.36
  4.7 0.1 copy.37
  4.8 0.0 copy-done.7
  4.8 1.6 %fusion.1 = bf16[4,256,192]{2,1,0:T(8,128)(2,1)S(1)} fusion(bf16[4,256,32]{2,1,0:T(8,128)(2,1)} %bitcast.42, bf16[4,256,32]{2,1,0:T(8,128)(2,1)} %bitcast.41, bf16[4,256,128]{2,1,0:T(8,128)(2,1)S(1)} %dynamic-slice_bitcast_fusion, f32[4,256]{1,0:T(4,128)S(1)} %bitcast.47, s32[4,256]{1,0:T(4,128)S(1)} %bitcast.46, bf16[64,32]{1,0:T(8,128)(2,1)S(1)} %bitcast.45, ...), kind=kOutput, calls=%fused_computation.2 | convolution fusion | flops 27074560 | bytes 819200 | tf_op jit(solution)/shard_map/dot_general | solution.py:517
  6.5 0.9 maximum_maximum_fusion.wq
  7.4 0.0 copy-done.5
  7.4 0.1 pad.3.clone
  7.4 0.0 copy-done.6
  7.5 0.6 fusion.7.bias
  8.1 0.0 copy-done.1
  8.1 1.3 copy.22
  9.4 132.5 %shard_map.130 = (bf16[32,8192]{1,0:T(8,128)(2,1)}, bf16[4,8,32,128]{3,2,1,0:T(8,128)(2,1)}, bf16[2,4,8,32,32]{4,3,2,1,0:T(8,128)(2,1)}) custom-call(bf16[4,8,32,480]{3,2,1,0:T(8,128)(2,1)} %bitcast.37, bf16[32,8192]{1,0:T(8,128)(2,1)} %res.1, bf16[480,8192]{1,0:T(8,128)(2,1)} %w.1, bf16[4,384,128]{2,1,0:T(8,128)(2,1)} %maximum_maximum_fusion.wq, ...), custom_call_target="tpu_custom_call" | custom-call | flops 12000000000 | bytes 14000000 | tf_op jit(solution)/shard_map/pallas_call | solution.py:532
  141.9 1.9 %copy.29 = bf16[2,1024,32]{1,2,0:T(8,128)(2,1)} copy(bf16[2,1024,32]{2,1,0:T(8,128)(2,1)} %bitcast.40) | data formatting | bytes 262144
  143.8 1.9 %copy.46 = bf16[32,8192]{1,0:T(8,128)(2,1)} copy(bf16[32,8192]{1,0:T(8,128)(2,1)} %get-tuple-element.28) | data formatting | bytes 1048576
  145.6 1.7 %copy.47 = bf16[1024,128]{1,0:T(8,128)(2,1)} copy(bf16[1024,128]{1,0:T(8,128)(2,1)} %bitcast.43) | data formatting | bytes 524288
  (12 shorter events, 0.2 us)
Async XLA Ops:
  0.6 3.8 %copy-start = (bf16[8192,128]{1,0:T(8,128)(2,1)S(1)}, bf16[8192,128]{1,0:T(8,128)(2,1)}, u32[]{:S(2)}) copy-start(bf16[8192,128]{1,0:T(8,128)(2,1)} %param.15) | copy-start | bytes 6291460
  2.1 2.4 %copy-start.2 = (s32[8192]{0:T(1024)S(1)}, s32[8192]{0:T(1024)}, u32[]{:S(2)}) copy-start(s32[8192]{0:T(1024)} %param.19) | copy-start | bytes 98308
  2.1 2.4 %copy-start.3 = (bf16[8192]{0:T(1024)(128)(2,1)S(1)}, bf16[8192]{0:T(1024)(128)(2,1)}, u32[]{:S(2)}) copy-start(bf16[8192]{0:T(1024)(128)(2,1)} %param.14) | copy-start | bytes 49156
  2.1 2.5 %copy-start.4 = (bf16[2,64,32]{1,2,0:T(8,128)(2,1)S(1)}, bf16[2,64,32]{1,2,0:T(8,128)(2,1)}, u32[]{:S(2)}) copy-start(bf16[2,64,32]{1,2,0:T(8,128)(2,1)} %param.18) | copy-start | bytes 24580
  2.1 2.7 %copy-start.7 = (bf16[64,128]{1,0:T(8,128)(2,1)S(1)}, bf16[64,128]{1,0:T(8,128)(2,1)}, u32[]{:S(2)}) copy-start(bf16[64,128]{1,0:T(8,128)(2,1)} %param.16) | copy-start | bytes 49156
  4.5 2.9 %copy-start.5 = (bf16[2,32]{1,0:T(2,128)(2,1)S(1)}, bf16[2,32]{1,0:T(2,128)(2,1)}, u32[]{:S(2)}) copy-start(bf16[2,32]{1,0:T(2,128)(2,1)} %param.21) | copy-start | bytes 388
  4.5 3.0 %copy-start.6 = (bf16[128]{0:T(256)(128)(2,1)S(1)}, bf16[128]{0:T(256)(128)(2,1)}, u32[]{:S(2)}) copy-start(bf16[128]{0:T(256)(128)(2,1)} %param.20) | copy-start | bytes 772
  4.5 3.6 %copy-start.1 = (bf16[1024,480]{0,1:T(8,128)(2,1)S(1)}, bf16[1024,480]{0,1:T(8,128)(2,1)}, u32[]{:S(2)}) copy-start(bf16[1024,480]{0,1:T(8,128)(2,1)} %param.11) | copy-start | bytes 2949124

commit v3 on v2

--- a/solution.py
+++ b/solution.py
@@ -13,16 +13,16 @@
 
 
 def kernel(
-    hid, res, w, wq, bias, nr_out, q_out, kv_out,
-    wb, hb, rsb, yb, wqp, kvw, part, snd, resb,
-    l_h, l_w, l_r, l_q, l_n,
+    hid, res, w, qcodes, pcodes, groups, gains, qscales, pscales, qbias, pbias, nr_out, q_out, kv_out,
+    wb, hb, rsb, yb, wq, qc, pc, wqp, kvw, part, snd, resb, gainf, ht,
+    l_h, l_w, l_r, l_q, l_n, l_c,
     h_s, h_r, w_s, w_r, wy_s, wy_r, wc_s, wc_r, q_s, q_r, qy_s, qy_r, qc_s, qc_r,
     r_s, r_r, rs_s, rs_r, ag_s, ag_r, n_s, n_r, p_s, p_r,
 ):
     t, d = lax.axis_index("tensor"), lax.axis_index("dp")
     x, z = t // NZ, t % NZ
     y, c = d // NC, d % NC
-    depth = hid.shape[-1]
+    depth = hid.shape[0]
     half = depth // 2
     cut = half // 32 * 16 + 16
 
@@ -53,12 +53,8 @@
 
     step_of = (1, 3)
 
-    def hid_local(u):
-        zl, zh = (z + 2 * NZ - 1 - u) % NZ, (z + 1 + u) % NZ
-        return (
-            pltpu.make_async_copy(hid.at[pl.ds(0, 2), zl], hb.at[0, u, pl.ds(0, 2)], l_h.at[u, 0]),
-            pltpu.make_async_copy(hid.at[pl.ds(2, 2), zh], hb.at[0, u, pl.ds(2, 2)], l_h.at[u, 1]),
-        )
+    def hid_local():
+        return pltpu.make_async_copy(hid, ht, l_h.at[0])
 
     def w_local(q, i):
         return pltpu.make_async_copy(
@@ -72,6 +68,13 @@
 
     def wq_local():
         return pltpu.make_async_copy(wq.at[x], wqp.at[0, rank], l_q.at[0])
+
+    def codes_local(o):
+        rows = pl.ds(pl.multiple_of(o * XW + rank * 256, 256), 256)
+        return (
+            pltpu.make_async_copy(qcodes.at[rows], qc.at[o], l_c.at[o, 0]),
+            pltpu.make_async_copy(pcodes.at[:, :, rows], pc.at[o], l_c.at[o, 1]),
+        )
 
     def nr_local(q):
         return pltpu.make_async_copy(
@@ -204,10 +207,17 @@
     others = (2, 1, 3)
 
     def h_send(u):
-        for copy in hid_local(u):
-            copy.wait()
         for side in range(2):
             h_direct(u, side).start()
+
+    def turn_hidden():
+        hid_local().wait()
+        for b in range(8):
+            turned = ht[:, b * 128 : (b + 1) * 128].astype(F32).T.astype(BF16)
+            for i in range(4):
+                xt, zc = b // 2, (b % 2) * 4 + i
+                u = (z + 2 * NZ - 1 - zc) % NZ if xt < 2 else (zc + 2 * NZ - 1 - z) % NZ
+                hb[0, u, xt] = turned[i * 32 : (i + 1) * 32]
 
     def h_pass(u):
         for side in range(2):
@@ -242,6 +252,27 @@
         for i in range(4):
             w_local(q, i).wait()
         w_c_in(q).wait_recv()
+
+    def scale_weights():
+        row = lax.broadcasted_iota(jnp.int32, (qscales.shape[0], 128), 0)
+        gainf[...] = gains[...].astype(F32)
+        for o in range(NX):
+            for copy in codes_local(o):
+                copy.wait()
+            picked = []
+            for j in range(2):
+                line = pl.ds(o * (XW // 128) + rank * 2 + j, 1)
+                picked.append(jnp.where(row == groups[line, :], gainf[line, :], 0.0).astype(BF16))
+            picked = jnp.concatenate(picked, axis=1)
+            factor = lax.dot_general(
+                picked, qscales[...], (((0,), (0,)), ((), ())), preferred_element_type=F32
+            )
+            wq[o, 0:256] = (qc[o].astype(F32) * factor).astype(BF16)
+            factor = jnp.dot(pscales[...].reshape(64, -1), picked, preferred_element_type=F32)
+            flat = pc[o].reshape(64, 256).astype(F32) * factor
+            packed = jnp.concatenate([flat[:, :128], flat[:, 128:]], axis=0)
+            wq[o, 256:384] = packed.T.astype(BF16)
+        wq_local().start()
 
     def reduce_step(q, k):
         acc = jnp.zeros((128, QW), F32)
@@ -318,24 +349,27 @@
             total += part[o - 1, k].astype(F32)
         lane = lax.broadcasted_iota(jnp.int32, (128, 256), 1)
         squares = jnp.sum(jnp.where((lane == 192) | (lane == 193), total, 0.0), axis=1, keepdims=True)
-        out = (total * lax.rsqrt(squares / (NX * XW) + 1e-6) + bias[...]).astype(BF16)
+        out = total * lax.rsqrt(squares / (NX * XW) + 1e-6)
+        wide_q = (out[:, :128] + qbias[...].astype(F32)).astype(BF16)
+        wide_k = (out[:, 128:160] + pbias[0:1, :].astype(F32)).astype(BF16)
+        wide_v = (out[:, 160:192] + pbias[1:2, :].astype(F32)).astype(BF16)
         for side in range(2):
             zz = (z + NZ - k) % NZ if side == 0 else (z + k) % NZ
             for i in range(2):
                 xt = 2 * side + i
-                rows = out[xt * 32 : (xt + 1) * 32]
-                q_out[xt, zz] = rows[:, :128]
-                kv_out[0, xt, zz] = rows[:, 128:160]
-                kv_out[1, xt, zz] = rows[:, 160:192]
-
-    for u in range(NZ):
-        for copy in hid_local(u):
-            copy.start()
+                rows = slice(xt * 32, (xt + 1) * 32)
+                q_out[xt, zz] = wide_q[rows]
+                kv_out[0, xt, zz] = wide_k[rows]
+                kv_out[1, xt, zz] = wide_v[rows]
+
+    hid_local().start()
     for q in range(NQ):
         for i in range(4):
             w_local(q, i).start()
     res_local().start()
-    wq_local().start()
+    for o in range(NX):
+        for copy in codes_local(o):
+            copy.start()
     for q in range(NQ):
         rsb[q, 0] = jnp.zeros(rsb.shape[2:], BF16)
 
@@ -346,7 +380,9 @@
     pl.semaphore_wait(barrier, len(friends))
 
     w_send(0)
+    turn_hidden()
     h_send(0)
+    scale_weights()
     w_spread(0)
     w_send(1)
     w_send(2)
@@ -504,23 +540,6 @@
     query_bias,
     pair_bias,
 ):
-    d = lax.axis_index("dp")
-    rank = (d % NC) * NY + d // NC
-    group_count = query_scales.shape[0]
-
-    def share(a):
-        return lax.dynamic_index_in_dim(a.reshape((NX, 8, 256) + a.shape[1:]), rank, 1, keepdims=False)
-
-    codes = jnp.concatenate([share(query_codes), share(pair_codes[0]), share(pair_codes[1])], axis=-1)
-    scales = jnp.concatenate([query_scales, pair_scales[0], pair_scales[1]], axis=-1)
-    selector = (share(input_groups)[..., None] == jnp.arange(group_count, dtype=jnp.int32)).astype(BF16)
-    scale_rows = jnp.dot(selector.reshape(1024, group_count), scales, preferred_element_type=F32)
-    scale_rows = scale_rows.reshape(codes.shape)
-    gain = share(norm_gain).astype(F32)[..., None]
-    wq = (codes.astype(F32) * scale_rows * gain).astype(BF16)
-    kv = jnp.concatenate([wq[:, :128, 128:], wq[:, 128:, 128:]], axis=-1)
-    wq = jnp.concatenate([wq[:, :, :128], kv], axis=1)
-    bias = jnp.concatenate([query_bias, pair_bias[0], pair_bias[1], jnp.zeros((64,), BF16)]).astype(F32)[None]
     depth = hidden.shape[1]
     dma = pltpu.SemaphoreType.DMA
     pairs = []
@@ -532,13 +551,13 @@
     new_residual, queries, key_values = pl.pallas_call(
         kernel,
         out_shape=(
-            jax.ShapeDtypeStruct(residual.shape, BF16),
-            jax.ShapeDtypeStruct((4, 8, 32, 128), BF16),
-            jax.ShapeDtypeStruct((2, 4, 8, 32, 32), BF16),
+            pltpu.VMEM(residual.shape, BF16),
+            pltpu.VMEM((4, 8, 32, 128), BF16),
+            pltpu.VMEM((2, 4, 8, 32, 32), BF16),
         ),
-        in_specs=[pl.BlockSpec(memory_space=pl.ANY)] * 4 + [pl.BlockSpec(memory_space=pltpu.VMEM)],
+        in_specs=[pl.BlockSpec(memory_space=pl.ANY)] * 5 + [pl.BlockSpec(memory_space=pltpu.VMEM)] * 6,
         out_specs=(
-            pl.BlockSpec(memory_space=pl.ANY),
+            pl.BlockSpec(memory_space=pltpu.VMEM),
             pl.BlockSpec(memory_space=pltpu.VMEM),
             pl.BlockSpec(memory_space=pltpu.VMEM),
         ),
@@ -547,18 +566,35 @@
             pltpu.VMEM((NX, NZ, 4, 32, depth), BF16),
             pltpu.VMEM((NQ, NZ, 4, 32, QW), BF16),
             pltpu.VMEM((NQ, NZ, 4, 32, QW), BF16),
+            pltpu.VMEM((NX, 384, 128), BF16),
+            pltpu.VMEM((NX, 256, 128), BF16),
+            pltpu.VMEM((NX, 2, 32, 256), BF16),
             pltpu.VMEM((NX, 8, 384, 128), BF16),
             pltpu.VMEM((XW, 256), BF16),
             pltpu.VMEM((3, NZ, 128, 256), BF16),
             pltpu.VMEM((NZ, NX, 128, 256), BF16),
             pltpu.VMEM((4, 32, XW), BF16),
-            dma((8, 2)), dma((NQ, 4)), dma((1,)), dma((1,)), dma((NQ,)),
+            pltpu.VMEM((NX * XW // 128, 128), F32),
+            pltpu.VMEM((depth, 1024), BF16),
+            dma((1,)), dma((NQ, 4)), dma((1,)), dma((1,)), dma((NQ,)), dma((NX, 2)),
         ] + pairs,
         compiler_params=pltpu.CompilerParams(
             collective_id=0, has_side_effects=True, vmem_limit_bytes=58 * 2**20
         ),
         cost_estimate=pl.CostEstimate(flops=12_000_000_000, bytes_accessed=14_000_000, transcendentals=0),
-    )(hidden.reshape(4, 8, 32, depth), residual, down_weight, wq, bias)
+    )(
+        hidden.T,
+        residual,
+        down_weight,
+        query_codes,
+        jnp.transpose(pair_codes, (0, 2, 1)),
+        input_groups.reshape(-1, 128),
+        norm_gain.reshape(-1, 128),
+        query_scales,
+        jnp.transpose(pair_scales, (0, 2, 1)),
+        query_bias.reshape(1, 128),
+        pair_bias,
+    )
     return new_residual, queries.reshape(1024, 128), key_values.reshape(2, 1024, 32)
 
 

time: 148 us -> 135 us (0.912)
  local copies, waits for them, and re-layouts: 10.9 us -> 2.34 us
  matrix products: 1.55 us -> 0 us
  other arithmetic: 1.51 us -> 0 us
    unnamed x28 -> x3, local copies, waits for them, and re-layouts: 8.96 us -> 2.34 us
    dot_general x1 -> x0, matrix products: 1.55 us -> none  [per_device(): jnp.dot(selector.reshape(1024, group_count), scales, preferred_element_ty...]
    slice x5 -> x0, local copies, waits for them, and re-layouts: 1.52 us -> none  [the longest x1 1.41 us: per_device(): pair_codes[0]]
where the time goes in v3:
time: 135 us
  Pallas kernels  132 us (98%)
  local copies, waits for them, and re-layouts  2.34 us (2%)
    pallas_call x1, Pallas kernels, per_device(): pl.pallas_call(kernel, out_shape=(pltpu.VMEM(residual.shape, BF16), pltpu...  132 us

profile of v3, /device:TPU:8, one launch (start us, length us, event | category | flops | bytes accessed | tf_op | source)
XLA Modules:
  0.0 135.0 jit_solution(13894860993403200107)
XLA Ops:
  0.6 132.0 %shard_map.130 = (bf16[32,8192]{1,0:T(8,128)(2,1)S(1)}, bf16[4,8,32,128]{3,2,1,0:T(8,128)(2,1)S(1)}, bf16[2,4,8,32,32]{4,3,2,1,0:T(8,128)(2,1)S(1)}) custom-call(bf16[480,1024]{1,0:T(8,128)(2,1)} %bitcast.11, bf16[32,8192]{1,0:T(8,128)(2,1)} %res.1, bf16[480,8192]{1,0:T(8,128)(2,1)} %w.1, bf16[8192,128]{1,0:T(8,128)(2,1)} %qcodes.1, ...), custom_call_target="tpu_custom_call" | custom-call | flops 12000000000 | bytes 14000000 | tf_op jit(solution)/shard_map/pallas_call | solution.py:551
  132.6 0.8 copy.17
  133.4 0.7 copy.18
  134.1 0.8 copy.14

commit v4 on v3

--- a/solution.py
+++ b/solution.py
@@ -29,14 +29,20 @@
     def at(xx, zz, yy, cc):
         return {"tensor": xx * NZ + zz, "dp": yy * NC + cc}
 
+    x_place = [(x + o) % NX for o in range(NX)]
+    y_place = [(y + o) % NY for o in range(NY)]
+    x_device = [at(p, z, y, c) for p in x_place]
+    y_device = [at(x, z, p, c) for p in y_place]
+    z_device = {o: at(x, (z + o + NZ) % NZ, y, c) for o in (1, -1)}
+
     def to_x(o):
-        return at((x + o) % NX, z, y, c)
+        return x_device[o % NX]
 
     def to_z(o):
-        return at(x, (z + o + NZ) % NZ, y, c)
+        return z_device[o]
 
     def to_y(o):
-        return at(x, z, (y + o) % NY, c)
+        return y_device[o % NY]
 
     sibling = at(x, z, y, 1 - c)
 
@@ -46,10 +52,10 @@
         )
 
     def xs(o):
-        return (x + o) % NX
+        return x_place[o % NX]
 
     def ys(o):
-        return (y + o) % NY
+        return y_place[o % NY]
 
     step_of = (1, 3)
 
@@ -214,6 +220,7 @@
         hid_local().wait()
         for b in range(8):
             turned = ht[:, b * 128 : (b + 1) * 128].astype(F32).T.astype(BF16)
+            turned = jnp.concatenate([turned, jnp.zeros((128, hb.shape[-1] - depth), BF16)], axis=1)
             for i in range(4):
                 xt, zc = b // 2, (b % 2) * 4 + i
                 u = (z + 2 * NZ - 1 - zc) % NZ if xt < 2 else (zc + 2 * NZ - 1 - z) % NZ
@@ -278,7 +285,7 @@
         acc = jnp.zeros((128, QW), F32)
         for o in range(NX):
             weight = jnp.concatenate([wb[q, o, i] for i in range(4)], axis=1)
-            acc += jnp.dot(hb[o, k].reshape(128, depth), weight, preferred_element_type=F32)
+            acc += jnp.dot(hb[o, k].reshape(128, hb.shape[-1])[:, :depth], weight, preferred_element_type=F32)
 
         @pl.when(k > 0)
         def _():
@@ -362,6 +369,10 @@
                 kv_out[0, xt, zz] = wide_k[rows]
                 kv_out[1, xt, zz] = wide_v[rows]
 
+    barrier = pltpu.get_barrier_semaphore()
+    friends = [to_x(1), to_x(2), to_x(3), to_z(1), to_z(-1), to_y(1), to_y(3), sibling]
+    for friend in friends:
+        pl.semaphore_signal(barrier, inc=1, device_id=friend, device_id_type=MESH)
     hid_local().start()
     for q in range(NQ):
         for i in range(4):
@@ -373,16 +384,11 @@
     for q in range(NQ):
         rsb[q, 0] = jnp.zeros(rsb.shape[2:], BF16)
 
-    barrier = pltpu.get_barrier_semaphore()
-    friends = [to_x(1), to_x(2), to_x(3), to_z(1), to_z(-1), to_y(1), to_y(3), sibling]
-    for friend in friends:
-        pl.semaphore_signal(barrier, inc=1, device_id=friend, device_id_type=MESH)
     pl.semaphore_wait(barrier, len(friends))
 
     w_send(0)
     turn_hidden()
     h_send(0)
-    scale_weights()
     w_spread(0)
     w_send(1)
     w_send(2)
@@ -440,6 +446,7 @@
 
         @pl.when(s == 3)
         def _():
+            scale_weights()
             for o in others:
                 q_x(o).start()
 
@@ -464,6 +471,32 @@
             for side in range(2):
                 q_forward_in(side).wait_recv()
             q_c().start()
+
+    def finish_quarter(q):
+        nr_local(q).wait()
+        for o in (1, 2, 3):
+            nr_x_in(q, o).wait_recv()
+            nr_x(q, o).wait_send()
+            w_x(q, o).wait_send()
+        for side in range(2):
+            w_y(q, side).wait_send()
+            w_forward(q, side).wait_send()
+        w_c(q).wait_send()
+
+    def finish_step(k):
+        for side in range(2):
+            h_direct(k, side).wait_send()
+            h_forward(k, side).wait_send()
+
+        @pl.loop(0, NQ)
+        def _(q):
+            for side in range(2):
+                ring(rsb, rs_s, rs_r, q, k, side).wait_send()
+                ring(yb, ag_s, ag_r, q, k, side).wait_send()
+
+    def finish_part(k):
+        for o in (1, 2, 3):
+            part_x(k, o).wait_send()
 
     q_c_in().wait_recv()
     for i in range(2 * NY):
@@ -486,45 +519,32 @@
         @pl.when(k >= 2)
         def _():
             combine_step(k - 2)
+            finish_part(k - 2)
+
+        @pl.when(k > 0)
+        def _():
+            finish_step(k - 1)
+
+        @pl.when((k > 1) & (k < NQ + 2))
+        def _():
+            finish_quarter(k - 2)
+
+        @pl.when(k == 1)
+        def _():
+            for o in (1, 2, 3):
+                q_x(o).wait_send()
+                res_x(o).wait_send()
+            for side in range(2):
+                q_y(side).wait_send()
+                q_forward(side).wait_send()
+                h_direct(NZ - 1, side).wait_send()
+                h_forward(NZ - 1, side).wait_send()
+            q_c().wait_send()
 
     @pl.loop(NZ - 2, NZ)
     def _(k):
         combine_step(k)
-
-    @pl.loop(0, NQ)
-    def _(q):
-        nr_local(q).wait()
-        for o in (1, 2, 3):
-            nr_x_in(q, o).wait_recv()
-            nr_x(q, o).wait_send()
-            w_x(q, o).wait_send()
-        for side in range(2):
-            w_y(q, side).wait_send()
-            w_forward(q, side).wait_send()
-        w_c(q).wait_send()
-
-    for o in (1, 2, 3):
-        q_x(o).wait_send()
-        res_x(o).wait_send()
-    for side in range(2):
-        q_y(side).wait_send()
-        q_forward(side).wait_send()
-    q_c().wait_send()
-
-    @pl.loop(0, NZ)
-    def _(k):
-        for side in range(2):
-            h_direct(k, side).wait_send()
-            h_forward(k, side).wait_send()
-        for o in (1, 2, 3):
-            part_x(k, o).wait_send()
-
-    @pl.loop(0, NZ - 1)
-    def _(k):
-        for q in range(NQ):
-            for side in range(2):
-                ring(rsb, rs_s, rs_r, q, k, side).wait_send()
-                ring(yb, ag_s, ag_r, q, k, side).wait_send()
+        finish_part(k)
 
 
 def per_device(
@@ -541,6 +561,7 @@
     pair_bias,
 ):
     depth = hidden.shape[1]
+    wide_depth = (depth + 127) // 128 * 128
     dma = pltpu.SemaphoreType.DMA
     pairs = []
     for shape in (
@@ -563,7 +584,7 @@
         ),
         scratch_shapes=[
             pltpu.VMEM((NQ, NX, 4, depth, 128), BF16),
-            pltpu.VMEM((NX, NZ, 4, 32, depth), BF16),
+            pltpu.VMEM((NX, NZ, 4, 32, wide_depth), BF16),
             pltpu.VMEM((NQ, NZ, 4, 32, QW), BF16),
             pltpu.VMEM((NQ, NZ, 4, 32, QW), BF16),
             pltpu.VMEM((NX, 384, 128), BF16),

time: 135 us -> 134 us (level)
  Pallas kernels: 132 us -> 130 us
    pallas_call x1, Pallas kernels: 132 us -> 130 us  [per_device(): pl.pallas_call(kernel, out_shape=(pltpu.VMEM(residual.shape, BF16), pltpu...]
where the time goes in v4:
time: 134 us; the launch traced here: 133 us
  Pallas kernels  130 us (97%)
  local copies, waits for them, and re-layouts  2.34 us (2%)
    pallas_call x1, Pallas kernels, per_device(): pl.pallas_call(kernel, out_shape=(pltpu.VMEM(residual.shape, BF16), pltpu...  130 us

profile of v4, /device:TPU:8, one launch (start us, length us, event | category | flops | bytes accessed | tf_op | source)
XLA Modules:
  0.0 133.4 jit_solution(6325328010029001470)
XLA Ops:
  0.6 130.4 %shard_map.130 = (bf16[32,8192]{1,0:T(8,128)(2,1)S(1)}, bf16[4,8,32,128]{3,2,1,0:T(8,128)(2,1)S(1)}, bf16[2,4,8,32,32]{4,3,2,1,0:T(8,128)(2,1)S(1)}) custom-call(bf16[480,1024]{1,0:T(8,128)(2,1)} %bitcast.11, bf16[32,8192]{1,0:T(8,128)(2,1)} %res.1, bf16[480,8192]{1,0:T(8,128)(2,1)} %w.1, bf16[8192,128]{1,0:T(8,128)(2,1)} %qcodes.1, ...), custom_call_target="tpu_custom_call" | custom-call | flops 12000000000 | bytes 14000000 | tf_op jit(solution)/shard_map/pallas_call | solution.py:572
  131.1 0.8 copy.17
  131.9 0.7 copy.18
  132.6 0.8 copy.14

commit v5 on v4

--- a/solution.py
+++ b/solution.py
@@ -424,13 +424,13 @@
 
             @pl.when(q <= s)
             def _():
-                reduce_step(q, jnp.where(s > 2 * q, s, jnp.maximum(2 * (s - q) - 1, 0)))
+                reduce_step(q, s - q + jnp.minimum(jnp.maximum(s - 4, 0), q))
 
         @pl.loop(1, NQ)
         def _(q):
-            @pl.when((q < s) & (s <= 2 * q))
+            @pl.when((s >= 4) & (s < q + 4))
             def _():
-                reduce_step(q, 2 * (s - q))
+                reduce_step(q, 2 * s - q - 4 + 1)
 
         @pl.when(s < NQ - 2)
         def _():

time: 134 us -> 133 us (level)
  no operation moved by 1% of the time
where the time goes in v5:
time: 133 us
  Pallas kernels  130 us (98%)
  local copies, waits for them, and re-layouts  2.34 us (2%)
    pallas_call x1, Pallas kernels, per_device(): pl.pallas_call(kernel, out_shape=(pltpu.VMEM(residual.shape, BF16), pltpu...  130 us

profile of v5, /device:TPU:8, one launch (start us, length us, event | category | flops | bytes accessed | tf_op | source)
XLA Modules:
  0.0 133.3 jit_solution(4036805972227359746)
XLA Ops:
  0.6 130.3 %shard_map.130 = (bf16[32,8192]{1,0:T(8,128)(2,1)S(1)}, bf16[4,8,32,128]{3,2,1,0:T(8,128)(2,1)S(1)}, bf16[2,4,8,32,32]{4,3,2,1,0:T(8,128)(2,1)S(1)}) custom-call(bf16[480,1024]{1,0:T(8,128)(2,1)} %bitcast.11, bf16[32,8192]{1,0:T(8,128)(2,1)} %res.1, bf16[480,8192]{1,0:T(8,128)(2,1)} %w.1, bf16[8192,128]{1,0:T(8,128)(2,1)} %qcodes.1, ...), custom_call_target="tpu_custom_call" | custom-call | flops 12000000000 | bytes 14000000 | tf_op jit(solution)/shard_map/pallas_call | solution.py:572
  130.9 0.8 copy.17
  131.7 0.7 copy.18
  132.4 0.8 copy.14
